TPU v7x, 32 devices: a whole 2x2x4 slice. The times are simulated.
32 devices in a mesh: cfg: 2 (over y), tm: 8 (over z, x), space: 2 (over core).
Axes of the slice: x: 2, y: 2, z: 4, core: 2. Of those that a mesh axis runs over, the one named last changes fastest.
Arguments:
- vectors: bfloat16 [16, 2, 3, 8, 4, 16, 128], P(('cfg', 'tm'), None, None, 'space'), parts along dimension 0, may hold values from -6 to 6
- gauge_links: float32 [16, 3, 2, 3, 3, 8, 4, 16], P(('cfg', 'tm'), None, None, None, None, 'space'), parts along dimension 0, may hold values from -2.5 to 2.5
- perambulators: bfloat16 [16, 8, 4, 128, 256], P(('cfg', 'tm')), parts along dimension 0, may hold values from -0.375 to 0.375
- momenta: int32 [8, 3], replicated, may hold values from -2 to 2
- displacements: int32 [8], replicated, may hold values from 0 to 3, as said below
Outputs:
- elementals: bfloat16 [16, 8, 128, 256], P(('cfg', 'tm'), None, 'space'), parts along dimension 0
- correlators: float32 [8, 16, 8], P(None, ('cfg', 'tm')), parts along dimension 1
There are 2 independent parts, one for each index of `cfg`. A program takes and returns all parts, laid end to end along the dimension named above; an argument that names none is the same for every part. Nothing has to cross between parts.
Inputs may be any that keep to these rules, and one draw needn't show every extreme that they name: `displacements`: each of the values 0, 1, 2, 3 appears exactly 2 times.
All inputs are finite; a program needn't handle non-finite values.
Results may differ from a plain program's by a relative error of at most 0.0075.
Values may be sent and summed in bfloat16 or wider, within the bound.
A program may use at most 64 MiB of HBM per device.

v0:
```python
import functools
import math

import jax
import jax.numpy as jnp
from jax import lax
from jax.experimental import pallas as pl
from jax.experimental.pallas import tpu as pltpu
from jax.sharding import PartitionSpec as P

F32 = jnp.float32
BF16 = jnp.bfloat16
MESH = pl.DeviceIdType.MESH


def combine(block, n):
    real = block[:n, :n] + block[n:, n:]
    imag = block[:n, n:] - block[n:, :n]
    return real, imag


def field_kernel(disp_ref, v_ref, before_ref, after_ref, links_ref, phase_ref, out_ref, pad, fields, left):
    _, _, nx, ny, nz, n = v_ref.shape
    ops = out_ref.shape[0]
    pad[:, :, 1 : nx + 1] = v_ref[...]
    pad[:, :, 0:1] = before_ref[...]
    pad[:, :, nx + 1 : nx + 2] = after_ref[...]

    def spread(table, column):
        return jnp.broadcast_to(table[:, column : column + 1], (nz, n))

    def load(x, y):
        return [[pad[r, c, x, y].astype(F32) for c in range(3)] for r in range(2)]

    def times(link, field, adjoint):
        real, imag = [], []
        for t in range(3):
            re, im = None, None
            for s in range(3):
                at = s * 3 + t if adjoint else t * 3 + s
                er, ei = link[at], link[9 + at]
                fr, fi = field[0][s], field[1][s]
                if adjoint:
                    a, b = er * fr + ei * fi, er * fi - ei * fr
                else:
                    a, b = er * fr - ei * fi, er * fi + ei * fr
                re = a if re is None else re + a
                im = b if im is None else im + b
            real.append(re)
            imag.append(im)
        return [real, imag]

    def rolled(field, shift):
        return [[pltpu.roll(e, shift, axis=0) for e in part] for part in field]

    def step(i, carry):
        x, y = i // ny, i % ny
        here = load(x + 1, y)
        table = links_ref[x + 1, y]
        back_x = links_ref[x, y]
        y_down = (y + ny - 1) % ny
        back_y = links_ref[x + 1, y_down]
        total = None

        def add(total, field):
            if total is None:
                return field
            return [[a + b for a, b in zip(p, q)] for p, q in zip(total, field)]

        for mu in range(3):
            link = [spread(table, mu * 18 + e) for e in range(18)]
            if mu == 0:
                ahead = load(x + 2, y)
            elif mu == 1:
                ahead = load(x + 1, (y + 1) % ny)
            else:
                ahead = rolled(here, nz - 1)
            forward = times(link, ahead, False)
            total = add(total, forward)
            for r in range(2):
                for c in range(3):
                    fields[mu + 1, c, i, :, r * n : (r + 1) * n] = forward[r][c].astype(BF16)
            if mu == 0:
                behind = [spread(back_x, e) for e in range(18)]
                backward = times(behind, load(x, y), True)
            elif mu == 1:
                behind = [spread(back_y, 18 + e) for e in range(18)]
                backward = times(behind, load(x + 1, y_down), True)
            else:
                backward = rolled(times(link, here, True), 1)
            total = add(total, backward)
        for r in range(2):
            for c in range(3):
                smooth = here[r][c] - total[r][c] / 6.0
                fields[0, c, i, :, r * n : (r + 1) * n] = smooth.astype(BF16)
        angles = phase_ref[x, y]
        for o in range(ops):
            cosine = spread(angles, o)
            sine = spread(angles, ops + o)
            for c in range(3):
                vr, vi = here[0][c], here[1][c]
                left[o, c, i, :, :n] = (vr * cosine - vi * sine).astype(BF16)
                left[o, c, i, :, n:] = (vr * sine + vi * cosine).astype(BF16)
        return carry

    lax.fori_loop(0, nx * ny, step, 0)
    rows = 3 * nx * ny * nz

    def project(o, carry):
        lhs = left[o].reshape(rows, 2 * n)
        rhs = fields[disp_ref[o]].reshape(rows, 2 * n)
        block = lax.dot_general(lhs, rhs, (((0,), (0,)), ((), ())), preferred_element_type=F32)
        real, imag = combine(block, n)
        out_ref[o, :, :n] = real
        out_ref[o, :, n:] = imag
        return carry

    lax.fori_loop(0, ops, project, 0)


def meson_kernel(
    count, norm, part_ref, per_ref, elem_ref, corr_ref,
    got, own, rows_in, ring, mixed, sand, acc, pair_send, pair_recv, send_sem, recv_sem,
):
    seps, spins, n, wide = per_ref.shape
    half = own.shape[0]
    mine_rows = elem_ref.shape[1]
    cfg, t, s = lax.axis_index("cfg"), lax.axis_index("tm"), lax.axis_index("space")
    other = 1 - s
    partner = (cfg, t, other)
    ringed = count == 8 and seps == 8
    if ringed:
        odd = t % 2
        place = (1 - odd) * (t // 2) + odd * ((15 - t) // 2)

        def at_place(p):
            p = (p + 16) % 8
            high = p // 4
            return (1 - high) * (2 * p) + high * (15 - 2 * p)

        targets = [at_place(place + 1), at_place(place - 1)]
        greet = list(targets)
    else:
        targets = [(t + d) % count for d in range(1, seps)]
        greet = targets + [(t + count - d) % count for d in range(1, seps)]

    barrier = pltpu.get_barrier_semaphore()
    pl.semaphore_signal(barrier, inc=1, device_id=partner, device_id_type=MESH)
    for g in greet:
        pl.semaphore_signal(barrier, inc=1, device_id=(cfg, g, s), device_id_type=MESH)
    pl.semaphore_wait(barrier, 1 + len(greet))

    def pair(src, dst, k):
        copy = pltpu.make_async_remote_copy(
            src_ref=src, dst_ref=dst, send_sem=pair_send.at[k], recv_sem=pair_recv.at[k],
            device_id=partner, device_id_type=MESH,
        )
        copy.start()
        return copy

    first = [pair(part_ref.at[other * half + o], got.at[o], o) for o in range(half)]

    if ringed:
        pieces = 2
        size = half // pieces

        def hop(way, k, g):
            span = pl.ds(g * size, size)
            src = own.at[span] if k == 0 else ring.at[way * 4 + k - 1, span]
            return pltpu.make_async_remote_copy(
                src_ref=src, dst_ref=ring.at[way * 4 + k, span],
                send_sem=send_sem.at[way, k, g], recv_sem=recv_sem.at[way, k, g],
                device_id=(cfg, targets[way], s), device_id_type=MESH,
            )

    hops = {}
    for o in range(half):
        first[o].wait_recv()
        own[o] = ((part_ref[s * half + o] + got[o]) * norm).astype(BF16)
        if ringed and (o + 1) % size == 0:
            for way in range(2):
                hops[way, 0, o // size] = hop(way, 0, o // size)
                hops[way, 0, o // size].start()
    if not ringed:
        for k in range(seps - 1):
            hops[k] = pltpu.make_async_remote_copy(
                src_ref=own, dst_ref=ring.at[k], send_sem=send_sem.at[k, 0, 0],
                recv_sem=recv_sem.at[k, 0, 0],
                device_id=(cfg, targets[k], s), device_id_type=MESH,
            )
            hops[k].start()
    rows_copy = pair(own.at[:, pl.ds(other * mine_rows, mine_rows)], rows_in, half)
    elem_ref[pl.ds(s * half, half)] = own[:, pl.ds(s * mine_rows, mine_rows)]

    def sandwich(d):
        flat = own[...].reshape(half * n, wide)
        for a in range(spins):
            spin = per_ref[d, a]
            turned = jnp.concatenate([-spin[:, n:], spin[:, :n]], axis=1)
            block = jnp.concatenate([spin, turned], axis=0)
            prod = jnp.dot(flat, block, preferred_element_type=F32).astype(BF16)
            for o in range(half):
                mixed[a * n : (a + 1) * n, o * wide : (o + 1) * wide] = prod[o * n : (o + 1) * n]
        lhs = per_ref[d].reshape(spins * n, wide).T
        for o in range(half):
            both = jnp.dot(lhs, mixed[:, o * wide : (o + 1) * wide], preferred_element_type=F32)
            real, imag = combine(both, n)
            sand[o, :, :n] = real
            sand[o, :, n:] = imag

    def contract(d, block):
        for o in range(half):
            term = jnp.sum(block[o].astype(F32) * sand[o], axis=0, keepdims=True)
            acc[s, d, pl.ds(o, 1)] = (term[:, :n] + term[:, n:]) * (1.0 / n)

    sandwich(0)
    contract(0, own)
    if ringed:
        for k in range(1, 5):
            for g in range(pieces):
                for way in range(2):
                    if (way, k - 1, g) not in hops or k == 4:
                        continue
                    hops[way, k - 1, g].wait_recv()
                    if k < 3 or g == way:
                        hops[way, k, g] = hop(way, k, g)
                        hops[way, k, g].start()
            if k < 4:
                for way in range(2):
                    source = at_place(place - k if way == 0 else place + k)
                    d = (t - source + 8) % 8
                    sandwich(d)
                    contract(d, ring.at[way * 4 + k - 1])
            else:
                d = (t - at_place(place + 4) + 8) % 8
                sandwich(d)
                hops[0, 3, 0].wait_recv()
                hops[1, 3, 1].wait_recv()
                for o in range(half):
                    way = o // size
                    term = jnp.sum(ring[way * 4 + 3, o].astype(F32) * sand[o], axis=0, keepdims=True)
                    acc[s, d, pl.ds(o, 1)] = (term[:, :n] + term[:, n:]) * (1.0 / n)
    else:
        for k in range(seps - 1):
            sandwich(k + 1)
            hops[k].wait_recv()
            contract(k + 1, ring.at[k])
    last = pair(acc.at[s], acc.at[s], half + 1)
    rows_copy.wait_recv()
    elem_ref[pl.ds(other * half, half)] = rows_in[...]
    for copy in hops.values():
        copy.wait_send()
    for copy in first:
        copy.wait_send()
    rows_copy.wait_send()
    last.wait()
    corr_ref[...] = acc[...]


def body(vectors, gauge_links, perambulators, momenta, displacements):
    space_index = lax.axis_index("space")
    space_count = lax.axis_size("space")
    count = lax.axis_size("tm")
    field = vectors[0]
    _, _, nx, ny, nz, n = field.shape
    ops = momenta.shape[0]
    up = [(i, (i + 1) % space_count) for i in range(space_count)]
    down = [(j, i) for i, j in up]
    before = lax.ppermute(field[:, :, nx - 1 :], "space", up)
    after = lax.ppermute(field[:, :, :1], "space", down)
    links = gauge_links[0]
    lower = lax.ppermute(links[0, :, :, :, nx - 1 :], "space", up)
    lower = jnp.concatenate([lower[None], jnp.zeros((2,) + lower.shape, F32)])
    links = jnp.concatenate([lower, links], axis=4)
    links = jnp.transpose(links.reshape(54, nx + 1, ny, nz), (1, 2, 3, 0))

    extent_x = nx * space_count
    xs = (space_index * nx + jnp.arange(nx, dtype=jnp.int32)).astype(F32)
    ys = jnp.arange(ny, dtype=jnp.int32).astype(F32)
    zs = jnp.arange(nz, dtype=jnp.int32).astype(F32)
    mom = momenta.astype(F32)
    angle = (mom[:, 0] * xs[:, None] / extent_x)[:, None, None, :]
    angle = angle + (mom[:, 1] * ys[:, None] / ny)[None, :, None, :]
    angle = angle + (mom[:, 2] * zs[:, None] / nz)[None, None, :, :]
    angle = 2.0 * math.pi * angle
    phases = jnp.concatenate([jnp.cos(angle), jnp.sin(angle)], axis=-1)

    vmem = pl.BlockSpec(memory_space=pltpu.VMEM)
    partial_value = pl.pallas_call(
        field_kernel,
        out_shape=jax.ShapeDtypeStruct((ops, n, 2 * n), F32),
        in_specs=[pl.BlockSpec(memory_space=pltpu.SMEM)] + [vmem] * 5,
        out_specs=vmem,
        scratch_shapes=[
            pltpu.VMEM((2, 3, nx + 2, ny, nz, n), BF16),
            pltpu.VMEM((4, 3, nx * ny, nz, 2 * n), BF16),
            pltpu.VMEM((ops, 3, nx * ny, nz, 2 * n), BF16),
        ],
        compiler_params=pltpu.CompilerParams(vmem_limit_bytes=40 * 2**20),
        name="fields",
    )(displacements, field, before, after, links, phases)

    perams = perambulators[0]
    seps, spins = perams.shape[:2]
    half = ops // 2
    norm = 1.0 / math.sqrt(6.0 * extent_x * ny * nz)
    elementals, corr = pl.pallas_call(
        functools.partial(meson_kernel, count, norm),
        out_shape=(
            jax.ShapeDtypeStruct((ops, n // 2, 2 * n), BF16),
            jax.ShapeDtypeStruct((2, seps, half, n), F32),
        ),
        in_specs=[vmem] * 2,
        out_specs=(vmem, vmem),
        scratch_shapes=[
            pltpu.VMEM((half, n, 2 * n), F32),
            pltpu.VMEM((half, n, 2 * n), BF16),
            pltpu.VMEM((half, n // 2, 2 * n), BF16),
            pltpu.VMEM((8, half, n, 2 * n), BF16),
            pltpu.VMEM((spins * n, half * 2 * n), BF16),
            pltpu.VMEM((half, n, 2 * n), F32),
            pltpu.VMEM((2, seps, half, n), F32),
            pltpu.SemaphoreType.DMA((half + 2,)),
            pltpu.SemaphoreType.DMA((half + 2,)),
            pltpu.SemaphoreType.DMA((8, 4, 2)),
            pltpu.SemaphoreType.DMA((8, 4, 2)),
        ],
        compiler_params=pltpu.CompilerParams(
            collective_id=0, has_side_effects=True, vmem_limit_bytes=40 * 2**20
        ),
        name="mesons",
    )(partial_value, perams)
    corr = jnp.sum(corr, axis=-1)
    corr = jnp.transpose(corr, (0, 2, 1)).reshape(ops, 1, seps)
    return (elementals[None], corr)


def solution(mesh):
    return jax.shard_map(
        body,
        mesh=mesh,
        in_specs=(
            P(("cfg", "tm"), None, None, "space", None, None, None),
            P(("cfg", "tm"), None, None, None, None, "space", None, None),
            P(("cfg", "tm"), None, None, None, None),
            P(),
            P(),
        ),
        out_specs=(P(("cfg", "tm"), None, "space", None), P(None, ("cfg", "tm"), None)),
        check_vma=False,
    )
```

profile of v0, /device:TPU:0, one launch (start us, length us, event | category | flops | bytes accessed | tf_op | source)
XLA Modules:
  0.0 48.6 jit_solution(5638576267770273017)
XLA Ops:
  0.6 0.0 copy-start.1
  0.6 0.0 copy-start.2
  0.7 0.8 %slice_bitcast_fusion = f32[2,3,3,1,4,16]{5,4,2,1,0,3:T(4,128)S(1)} fusion(f32[3,2,3,3,4,4,16]{6,5,4,3,2,1,0:T(4,128)} %bitcast.25), kind=kLoop, calls=%fused_computation.5 | loop fusion | bytes 9216 | tf_op jit(solution)/shard_map/squeeze | solution.py:272
  1.5 0.5 collective-permute-start.2
  1.9 0.0 copy-start
  1.9 1.1 %fusion.2 = (bf16[2,3,1,4,16,128]{5,4,3,2,1,0:T(8,128)(2,1)S(1)}, bf16[2,3,1,4,16,128]{5,4,3,2,1,0:T(8,128)(2,1)S(1)}) fusion(bf16[2,3,4,4,16,128]{5,4,3,2,1,0:T(8,128)(2,1)} %bitcast.22), kind=kLoop, calls=%fused_computation.16 | loop fusion | bytes 393216 | tf_op jit(solution)/shard_map/slice | solution.py:270
  3.0 0.1 collective-permute-start.1
  3.2 0.5 collective-permute-start
  3.6 0.7 %convert_element_type.24 = f32[8,3]{0,1:T(4,128)S(1)} convert(s32[8,3]{0,1:T(4,128)} %param.8) | non-fusion elementwise | flops 24 | bytes 192 | tf_op jit(solution)/shard_map/convert_element_type | solution.py:281
  4.3 0.1 multiply_multiply_fusion.1
  4.4 0.1 multiply_multiply_fusion
  4.5 0.5 fusion.1
  5.0 0.1 pad_maximum_fusion.phase_ref
  5.1 1.2 %copy.14 = f32[54,4,4,16]{0,3,2,1:T(8,128)S(1)} copy(f32[54,4,4,16]{3,2,1,0:T(4,128)} %bitcast.26) | data formatting | bytes 110592 | tf_op jit(solution)/shard_map/concatenate | solution.py:274
  6.3 0.0 collective-permute-done.2
  6.3 0.1 copy.13
  6.4 0.0 collective-permute-done.1.after_ref
  6.5 0.0 collective-permute-done.before_ref
  6.5 0.0 copy-done.1
  6.5 0.0 copy-done.2
  6.5 10.0 %fields.1.part_ref = f32[8,128,256]{2,1,0:T(8,128)S(1)} custom-call(s32[8]{0:T(128)S(1)} %copy-done.2, bf16[2,3,4,4,16,128]{5,4,3,2,1,0:T(8,128)(2,1)S(1)} %bitcast.23, bf16[2,3,1,4,16,128]{5,4,3,2,1,0:T(8,128)(2,1)S(1)} %collective-permute-done.before_ref, bf16[2,3,1,4,16,128]{5,4,3,2,1,0:T(8,128)(2,1)S(1)} %collective-permute-done.1.after_ref, ...), custom_call_target="tpu_custom_call" | custom-call | tf_op jit(solution)/shard_map/fields/pallas_call | solution.py:289
  16.5 0.0 copy-done
  16.5 30.5 %mesons.1 = (bf16[8,64,256]{2,1,0:T(8,128)(2,1)S(1)}, f32[2,8,4,128]{3,2,1,0:T(4,128)S(1)}) custom-call(f32[8,128,256]{2,1,0:T(8,128)S(1)} %fields.1.part_ref, bf16[8,4,128,256]{3,2,1,0:T(8,128)(2,1)S(1)} %bitcast.21), custom_call_target="tpu_custom_call" | custom-call | tf_op jit(solution)/shard_map/mesons/pallas_call | solution.py:307
  47.1 0.1 reduce_sum.9
  47.2 0.7 %copy.15 = f32[2,4,8]{2,1,0:T(4,128)} copy(f32[2,4,8]{1,2,0:T(8,128)S(1)} %bitcast.29) | data formatting | bytes 512 | tf_op jit(solution)/shard_map/transpose | solution.py:334
  47.9 0.7 %copy.18 = bf16[1,8,64,256]{3,2,1,0:T(8,128)(2,1)} copy(bf16[1,8,64,256]{3,2,1,0:T(8,128)(2,1)S(1)} %bitcast.24) | data formatting | bytes 524288
  (7 shorter events, 0.1 us)
Async XLA Ops:
  0.6 5.8 %copy-start.1 = (bf16[1,2,3,4,4,16,128]{6,5,4,3,2,1,0:T(8,128)(2,1)S(1)}, bf16[1,2,3,4,4,16,128]{6,5,4,3,2,1,0:T(8,128)(2,1)}, u32[]{:S(2)}) copy-start(bf16[1,2,3,4,4,16,128]{6,5,4,3,2,1,0:T(8,128)(2,1)} %param.5) | copy-start | bytes 1179652
  0.6 5.8 %copy-start.2 = (s32[8]{0:T(128)S(1)}, s32[8]{0:T(128)}, u32[]{:S(2)}) copy-start(s32[8]{0:T(128)} %disp_ref.1) | copy-start | bytes 100
  1.5 4.8 %collective-permute-start.2 = (f32[2,3,3,1,4,16]{5,4,2,1,0,3:T(4,128)S(1)}, f32[2,3,3,1,4,16]{5,4,2,1,0,3:T(4,128)S(1)}, u32[]{:S(2)}, u32[]{:S(2)}) collective-permute-start(f32[2,3,3,1,4,16]{5,4,2,1,0,3:T(4,128)S(1)} %slice_bitcast_fusion), channel_id=1, source_target_pairs={{0,1},{1,0},{2,3},{3,2},{4,5},{5,4},{6,7},{7,6},{8,9},{9,8},{10,11... | collective-permute-start | bytes 13832 | tf_op jit(solution)/shard_map/ppermute | solution.py:272
  1.9 14.6 %copy-start = (bf16[1,8,4,128,256]{4,3,2,1,0:T(8,128)(2,1)S(1)}, bf16[1,8,4,128,256]{4,3,2,1,0:T(8,128)(2,1)}, u32[]{:S(2)}) copy-start(bf16[1,8,4,128,256]{4,3,2,1,0:T(8,128)(2,1)} %param.7) | copy-start | bytes 6291460
  3.0 3.4 %collective-permute-start.1 = (bf16[2,3,1,4,16,128]{5,4,3,2,1,0:T(8,128)(2,1)S(1)}, bf16[2,3,1,4,16,128]{5,4,3,2,1,0:T(8,128)(2,1)S(1)}, u32[]{:S(2)}, u32[]{:S(2)}) collective-permute-start(bf16[2,3,1,4,16,128]{5,4,3,2,1,0:T(8,128)(2,1)S(1)} %get-tuple-element.12), channel_id=1, source_target_pairs={{1,0},{0,1},{3,2},{2,3},{5,4},{4,5},{7,6},{6,7},{9,8},{8,9},{11,10... | collective-permute-start | bytes 294920 | tf_op jit(solution)/shard_map/ppermute | solution.py:270
  3.2 3.3 %collective-permute-start = (bf16[2,3,1,4,16,128]{5,4,3,2,1,0:T(8,128)(2,1)S(1)}, bf16[2,3,1,4,16,128]{5,4,3,2,1,0:T(8,128)(2,1)S(1)}, u32[]{:S(2)}, u32[]{:S(2)}) collective-permute-start(bf16[2,3,1,4,16,128]{5,4,3,2,1,0:T(8,128)(2,1)S(1)} %get-tuple-element.13), channel_id=1, source_target_pairs={{0,1},{1,0},{2,3},{3,2},{4,5},{5,4},{6,7},{7,6},{8,9},{9,8},{10,11... | collective-permute-start | bytes 294920 | tf_op jit(solution)/shard_map/ppermute | solution.py:269
where the time goes:
time: 48.8 us; the launch traced here: 48.6 us
  Pallas kernels  40.6 us (83%)
  local copies, waits for them, and re-layouts  4.68 us (10%)
  other arithmetic  1.53 us (3%)
  starting transfers between devices  1.03 us (2%)
  between operations  0.74 us (2%)
    pallas_call x1, Pallas kernels, body(): pl.pallas_call(functools.partial(meson_kernel, count, norm), out_shape=(j...  30.5 us
    pallas_call x1, Pallas kernels, body(): pl.pallas_call(field_kernel, out_shape=jax.ShapeDtypeStruct((ops, n, 2 *...  10 us
    concatenate x2, local copies, waits for them, and re-layouts, body(): links = jnp.concatenate([lower, links], axis=4)  1.34 us
    slice x1, local copies, waits for them, and re-layouts, body(): after = lax.ppermute(field[:, :, :1], 'space', down)  1.1 us
  transfers between devices with their start and end apart: 3, of which 0 were waited for; matrix products, arithmetic and copies ran while one was open for 8% of the time, Pallas kernels for 0%

commit v1 on v0

--- a/solution.py
+++ b/solution.py
@@ -19,12 +19,9 @@
     return real, imag
 
 
-def field_kernel(disp_ref, v_ref, before_ref, after_ref, links_ref, phase_ref, out_ref, pad, fields, left):
+def make_fields(ready, v_ref, phase_ref, links_ref, pad, fields, left):
     _, _, nx, ny, nz, n = v_ref.shape
-    ops = out_ref.shape[0]
-    pad[:, :, 1 : nx + 1] = v_ref[...]
-    pad[:, :, 0:1] = before_ref[...]
-    pad[:, :, nx + 1 : nx + 2] = after_ref[...]
+    ops = left.shape[0]
 
     def spread(table, column):
         return jnp.broadcast_to(table[:, column : column + 1], (nz, n))
@@ -93,34 +90,28 @@
             for c in range(3):
                 smooth = here[r][c] - total[r][c] / 6.0
                 fields[0, c, i, :, r * n : (r + 1) * n] = smooth.astype(BF16)
+        return carry
+
+    def rotate(i, carry):
+        x, y = i // ny, i % ny
         angles = phase_ref[x, y]
         for o in range(ops):
             cosine = spread(angles, o)
             sine = spread(angles, ops + o)
             for c in range(3):
-                vr, vi = here[0][c], here[1][c]
+                vr, vi = v_ref[0, c, x, y].astype(F32), v_ref[1, c, x, y].astype(F32)
                 left[o, c, i, :, :n] = (vr * cosine - vi * sine).astype(BF16)
                 left[o, c, i, :, n:] = (vr * sine + vi * cosine).astype(BF16)
         return carry
 
+    lax.fori_loop(0, nx * ny, rotate, 0)
+    ready()
     lax.fori_loop(0, nx * ny, step, 0)
-    rows = 3 * nx * ny * nz
-
-    def project(o, carry):
-        lhs = left[o].reshape(rows, 2 * n)
-        rhs = fields[disp_ref[o]].reshape(rows, 2 * n)
-        block = lax.dot_general(lhs, rhs, (((0,), (0,)), ((), ())), preferred_element_type=F32)
-        real, imag = combine(block, n)
-        out_ref[o, :, :n] = real
-        out_ref[o, :, n:] = imag
-        return carry
-
-    lax.fori_loop(0, ops, project, 0)
 
 
 def meson_kernel(
-    count, norm, part_ref, per_ref, elem_ref, corr_ref,
-    got, own, rows_in, ring, mixed, sand, acc, pair_send, pair_recv, send_sem, recv_sem,
+    count, norm, disp_ref, v_ref, link_ref, phase_ref, per_ref, elem_ref, corr_ref,
+    pad, links, fields, left, part, got, own, rows_in, ring, mixed, sand, acc, pair_send, pair_recv, send_sem, recv_sem,
 ):
     seps, spins, n, wide = per_ref.shape
     half = own.shape[0]
@@ -158,7 +149,32 @@
         copy.start()
         return copy
 
-    first = [pair(part_ref.at[other * half + o], got.at[o], o) for o in range(half)]
+    nx = v_ref.shape[2]
+    rows = fields.shape[1] * fields.shape[2] * fields.shape[3]
+    halo = [
+        pair(v_ref.at[:, :, nx - 1], pad.at[:, :, 0], half + 2),
+        pair(v_ref.at[:, :, 0], pad.at[:, :, nx + 1], half + 3),
+        pair(link_ref.at[nx - 1], links.at[0], half + 4),
+    ]
+    pad[:, :, 1 : nx + 1] = v_ref[...]
+    links[1:] = link_ref[...]
+
+    def ready():
+        for copy in halo:
+            copy.wait_recv()
+
+    make_fields(ready, v_ref, phase_ref, links, pad, fields, left)
+
+    def project(o):
+        lhs = left[o].reshape(rows, wide)
+        rhs = fields[disp_ref[o]].reshape(rows, wide)
+        block = lax.dot_general(lhs, rhs, (((0,), (0,)), ((), ())), preferred_element_type=F32)
+        return combine(block, n)
+
+    first = []
+    for o in range(half):
+        part[o, :, :n], part[o, :, n:] = project(other * half + o)
+        first.append(pair(part.at[o], got.at[o], o))
 
     if ringed:
         pieces = 2
@@ -175,8 +191,10 @@
 
     hops = {}
     for o in range(half):
+        real, imag = project(s * half + o)
         first[o].wait_recv()
-        own[o] = ((part_ref[s * half + o] + got[o]) * norm).astype(BF16)
+        own[o, :, :n] = ((real + got[o, :, :n]) * norm).astype(BF16)
+        own[o, :, n:] = ((imag + got[o, :, n:]) * norm).astype(BF16)
         if ringed and (o + 1) % size == 0:
             for way in range(2):
                 hops[way, 0, o // size] = hop(way, 0, o // size)
@@ -250,7 +268,7 @@
     elem_ref[pl.ds(other * half, half)] = rows_in[...]
     for copy in hops.values():
         copy.wait_send()
-    for copy in first:
+    for copy in halo + first:
         copy.wait_send()
     rows_copy.wait_send()
     last.wait()
@@ -264,15 +282,8 @@
     field = vectors[0]
     _, _, nx, ny, nz, n = field.shape
     ops = momenta.shape[0]
-    up = [(i, (i + 1) % space_count) for i in range(space_count)]
-    down = [(j, i) for i, j in up]
-    before = lax.ppermute(field[:, :, nx - 1 :], "space", up)
-    after = lax.ppermute(field[:, :, :1], "space", down)
     links = gauge_links[0]
-    lower = lax.ppermute(links[0, :, :, :, nx - 1 :], "space", up)
-    lower = jnp.concatenate([lower[None], jnp.zeros((2,) + lower.shape, F32)])
-    links = jnp.concatenate([lower, links], axis=4)
-    links = jnp.transpose(links.reshape(54, nx + 1, ny, nz), (1, 2, 3, 0))
+    links = jnp.transpose(links.reshape(54, nx, ny, nz), (1, 2, 3, 0))
 
     extent_x = nx * space_count
     xs = (space_index * nx + jnp.arange(nx, dtype=jnp.int32)).astype(F32)
@@ -286,20 +297,6 @@
     phases = jnp.concatenate([jnp.cos(angle), jnp.sin(angle)], axis=-1)
 
     vmem = pl.BlockSpec(memory_space=pltpu.VMEM)
-    partial_value = pl.pallas_call(
-        field_kernel,
-        out_shape=jax.ShapeDtypeStruct((ops, n, 2 * n), F32),
-        in_specs=[pl.BlockSpec(memory_space=pltpu.SMEM)] + [vmem] * 5,
-        out_specs=vmem,
-        scratch_shapes=[
-            pltpu.VMEM((2, 3, nx + 2, ny, nz, n), BF16),
-            pltpu.VMEM((4, 3, nx * ny, nz, 2 * n), BF16),
-            pltpu.VMEM((ops, 3, nx * ny, nz, 2 * n), BF16),
-        ],
-        compiler_params=pltpu.CompilerParams(vmem_limit_bytes=40 * 2**20),
-        name="fields",
-    )(displacements, field, before, after, links, phases)
-
     perams = perambulators[0]
     seps, spins = perams.shape[:2]
     half = ops // 2
@@ -310,9 +307,14 @@
             jax.ShapeDtypeStruct((ops, n // 2, 2 * n), BF16),
             jax.ShapeDtypeStruct((2, seps, half, n), F32),
         ),
-        in_specs=[vmem] * 2,
+        in_specs=[pl.BlockSpec(memory_space=pltpu.SMEM)] + [vmem] * 4,
         out_specs=(vmem, vmem),
         scratch_shapes=[
+            pltpu.VMEM((2, 3, nx + 2, ny, nz, n), BF16),
+            pltpu.VMEM((nx + 1, ny, nz, 54), F32),
+            pltpu.VMEM((4, 3, nx * ny, nz, 2 * n), BF16),
+            pltpu.VMEM((ops, 3, nx * ny, nz, 2 * n), BF16),
+            pltpu.VMEM((half, n, 2 * n), F32),
             pltpu.VMEM((half, n, 2 * n), F32),
             pltpu.VMEM((half, n, 2 * n), BF16),
             pltpu.VMEM((half, n // 2, 2 * n), BF16),
@@ -320,8 +322,8 @@
             pltpu.VMEM((spins * n, half * 2 * n), BF16),
             pltpu.VMEM((half, n, 2 * n), F32),
             pltpu.VMEM((2, seps, half, n), F32),
-            pltpu.SemaphoreType.DMA((half + 2,)),
-            pltpu.SemaphoreType.DMA((half + 2,)),
+            pltpu.SemaphoreType.DMA((half + 5,)),
+            pltpu.SemaphoreType.DMA((half + 5,)),
             pltpu.SemaphoreType.DMA((8, 4, 2)),
             pltpu.SemaphoreType.DMA((8, 4, 2)),
         ],
@@ -329,7 +331,7 @@
             collective_id=0, has_side_effects=True, vmem_limit_bytes=40 * 2**20
         ),
         name="mesons",
-    )(partial_value, perams)
+    )(displacements, field, links, phases, perams)
     corr = jnp.sum(corr, axis=-1)
     corr = jnp.transpose(corr, (0, 2, 1)).reshape(ops, 1, seps)
     return (elementals[None], corr)

time: 48.8 us -> 48.6 us (level)
  local copies, waits for them, and re-layouts: 4.68 us -> 5.86 us
  starting transfers between devices: 1.03 us -> 0 us
    pallas_call x1 -> x0, Pallas kernels: 10 us -> none  [body(): pl.pallas_call(field_kernel, out_shape=jax.ShapeDtypeStruct((ops, n, 2 *...]
    pallas_call x1, Pallas kernels: 30.5 us -> 40.3 us  [body(): pl.pallas_call(functools.partial(meson_kernel, count, norm), out_shape=(j...]
    unnamed x7, local copies, waits for them, and re-layouts: 0.72 us -> 3.94 us
    concatenate x3 -> x0, local copies, waits for them, and re-layouts: 1.36 us -> none  [the longest x2 1.34 us: body(): links = jnp.concatenate([lower, links], axis=4)]
    another operation x0 -> x1, local copies, waits for them, and re-layouts: none -> 1.24 us  [body(): links = jnp.transpose(links.reshape(54, nx, ny, nz), (1, 2, 3, 0))]
    slice x1 -> x0, local copies, waits for them, and re-layouts: 1.1 us -> none  [body(): after = lax.ppermute(field[:, :, :1], 'space', down)]
    ppermute x3 -> x0, starting transfers between devices: 1.03 us -> none  [the longest x1 0.45 us: body(): before = lax.ppermute(field[:, :, nx - 1:], 'space', up)]
    squeeze x1 -> x0, local copies, waits for them, and re-layouts: 0.82 us -> none  [body(): lower = lax.ppermute(links[0, :, :, :, nx - 1:], 'space', up)]
  transfers between devices with their start and end apart: 3 -> 0, of which waited for: 0 -> 0; matrix products, arithmetic and copies ran while one was open for 8% -> 0% of each run, Pallas kernels for 0% -> 0%
where the time goes in v1:
time: 48.6 us; the launch traced here: 48.3 us
  Pallas kernels  40.3 us (83%)
  local copies, waits for them, and re-layouts  5.86 us (12%)
  other arithmetic  1.51 us (3%)
  between operations  0.69 us (1%)
    pallas_call x1, Pallas kernels, body(): pl.pallas_call(functools.partial(meson_kernel, count, norm), out_shape=(j...  40.3 us
    unnamed x7, local copies, waits for them, and re-layouts  3.94 us
    another operation x1, local copies, waits for them, and re-layouts, body(): links = jnp.transpose(links.reshape(54, nx, ny, nz), (1, 2, 3, 0))  1.24 us

profile of v1, /device:TPU:0, one launch (start us, length us, event | category | flops | bytes accessed | tf_op | source)
XLA Modules:
  0.0 48.3 jit_solution(15720852309479324600)
XLA Ops:
  0.7 0.7 %convert_element_type.24 = f32[8,3]{0,1:T(4,128)S(1)} convert(s32[8,3]{0,1:T(4,128)} %param.8) | non-fusion elementwise | flops 24 | bytes 192 | tf_op jit(solution)/shard_map/convert_element_type | solution.py:292
  1.4 0.1 multiply_multiply_fusion.1
  1.4 0.1 multiply_multiply_fusion
  1.5 1.2 %copy.11 = f32[54,4,4,16]{0,3,2,1:T(8,128)S(1)} copy(f32[54,4,4,16]{3,2,1,0:T(4,128)} %bitcast.19) | data formatting | bytes 110592 | tf_op jit(solution)/shard_map/reshape;squeeze | solution.py:286
  2.8 0.5 fusion.1
  3.2 0.1 pad_maximum_fusion.phase_ref
  3.3 0.0 copy-start
  3.4 1.6 %copy-done = bf16[1,8,4,128,256]{4,3,2,1,0:T(8,128)(2,1)S(1)} copy-done((bf16[1,8,4,128,256]{4,3,2,1,0:T(8,128)(2,1)S(1)}, bf16[1,8,4,128,256]{4,3,2,1,0:T(8,128)(2,1)}, u32[]{:S(2)}) %copy-start) | copy-done | bytes 2097176
  4.9 0.0 copy-start.1
  4.9 1.0 %copy-done.1 = bf16[1,2,3,4,4,16,128]{6,5,4,3,2,1,0:T(8,128)(2,1)S(1)} copy-done((bf16[1,2,3,4,4,16,128]{6,5,4,3,2,1,0:T(8,128)(2,1)S(1)}, bf16[1,2,3,4,4,16,128]{6,5,4,3,2,1,0:T(8,128)(2,1)}, u32[]{:S(2)}) %copy-start.1) | copy-done | bytes 393240
  5.9 0.0 copy-start.2
  5.9 0.7 %copy-done.2 = s32[8]{0:T(128)S(1)} copy-done((s32[8]{0:T(128)S(1)}, s32[8]{0:T(128)}, u32[]{:S(2)}) %copy-start.2) | copy-done | bytes 56
  6.6 40.3 %mesons.1 = (bf16[8,64,256]{2,1,0:T(8,128)(2,1)S(1)}, f32[2,8,4,128]{3,2,1,0:T(4,128)S(1)}) custom-call(s32[8]{0:T(128)S(1)} %copy-done.2, bf16[2,3,4,4,16,128]{5,4,3,2,1,0:T(8,128)(2,1)S(1)} %bitcast.17, f32[4,4,16,54]{3,2,1,0:T(8,128)S(1)} %bitcast.16, f32[4,4,16,16]{3,2,1,0:T(8,128)S(1)} %pad_maximum_fusion.phase_ref, bf16[8,4,128,256]{3,2,1,0:T(8,128)(2,1)S(1)} %bitcast.15), custom_call_target="tpu_custom_call" | custom-call | tf_op jit(solution)/shard_map/mesons/pallas_call | solution.py:304
  46.9 0.1 reduce_sum.9
  47.0 0.7 %copy.12 = f32[2,4,8]{2,1,0:T(4,128)} copy(f32[2,4,8]{1,2,0:T(8,128)S(1)} %bitcast.20) | data formatting | bytes 512 | tf_op jit(solution)/shard_map/transpose | solution.py:336
  47.6 0.7 %copy.15 = bf16[1,8,64,256]{3,2,1,0:T(8,128)(2,1)} copy(bf16[1,8,64,256]{3,2,1,0:T(8,128)(2,1)S(1)} %bitcast.18) | data formatting | bytes 524288
  (5 shorter events, 0.0 us)
Async XLA Ops:
  3.3 1.6 %copy-start = (bf16[1,8,4,128,256]{4,3,2,1,0:T(8,128)(2,1)S(1)}, bf16[1,8,4,128,256]{4,3,2,1,0:T(8,128)(2,1)}, u32[]{:S(2)}) copy-start(bf16[1,8,4,128,256]{4,3,2,1,0:T(8,128)(2,1)} %param.7) | copy-start | bytes 6291460
  4.9 1.0 %copy-start.1 = (bf16[1,2,3,4,4,16,128]{6,5,4,3,2,1,0:T(8,128)(2,1)S(1)}, bf16[1,2,3,4,4,16,128]{6,5,4,3,2,1,0:T(8,128)(2,1)}, u32[]{:S(2)}) copy-start(bf16[1,2,3,4,4,16,128]{6,5,4,3,2,1,0:T(8,128)(2,1)} %param.5) | copy-start | bytes 1179652
  5.9 0.7 %copy-start.2 = (s32[8]{0:T(128)S(1)}, s32[8]{0:T(128)}, u32[]{:S(2)}) copy-start(s32[8]{0:T(128)} %disp_ref.1) | copy-start | bytes 100

commit v2 on v1

--- a/solution.py
+++ b/solution.py
@@ -110,10 +110,12 @@
 
 
 def meson_kernel(
-    count, norm, disp_ref, v_ref, link_ref, phase_ref, per_ref, elem_ref, corr_ref,
-    pad, links, fields, left, part, got, own, rows_in, ring, mixed, sand, acc, pair_send, pair_recv, send_sem, recv_sem,
+    count, norm, disp_ref, v_ref, link_ref, phase_ref, per_hbm, elem_ref, corr_ref,
+    pad, links, fields, left, part, got, own, rows_in, ring, mixed, sand, acc, per_ref, per_sem, pair_send, pair_recv, send_sem, recv_sem,
 ):
     seps, spins, n, wide = per_ref.shape
+    fetch = pltpu.make_async_copy(per_hbm, per_ref, per_sem)
+    fetch.start()
     half = own.shape[0]
     mine_rows = elem_ref.shape[1]
     cfg, t, s = lax.axis_index("cfg"), lax.axis_index("tm"), lax.axis_index("space")
@@ -172,12 +174,15 @@
         return combine(block, n)
 
     first = []
-    for o in range(half):
+
+    def project_other(o):
         part[o, :, :n], part[o, :, n:] = project(other * half + o)
         first.append(pair(part.at[o], got.at[o], o))
 
+    project_other(0)
+
     if ringed:
-        pieces = 2
+        pieces = half
         size = half // pieces
 
         def hop(way, k, g):
@@ -191,6 +196,8 @@
 
     hops = {}
     for o in range(half):
+        if o + 1 < half:
+            project_other(o + 1)
         real, imag = project(s * half + o)
         first[o].wait_recv()
         own[o, :, :n] = ((real + got[o, :, :n]) * norm).astype(BF16)
@@ -231,6 +238,7 @@
             term = jnp.sum(block[o].astype(F32) * sand[o], axis=0, keepdims=True)
             acc[s, d, pl.ds(o, 1)] = (term[:, :n] + term[:, n:]) * (1.0 / n)
 
+    fetch.wait()
     sandwich(0)
     contract(0, own)
     if ringed:
@@ -240,7 +248,7 @@
                     if (way, k - 1, g) not in hops or k == 4:
                         continue
                     hops[way, k - 1, g].wait_recv()
-                    if k < 3 or g == way:
+                    if k < 3 or g // 2 == way:
                         hops[way, k, g] = hop(way, k, g)
                         hops[way, k, g].start()
             if k < 4:
@@ -252,10 +260,9 @@
             else:
                 d = (t - at_place(place + 4) + 8) % 8
                 sandwich(d)
-                hops[0, 3, 0].wait_recv()
-                hops[1, 3, 1].wait_recv()
                 for o in range(half):
-                    way = o // size
+                    way = o // 2
+                    hops[way, 3, o].wait_recv()
                     term = jnp.sum(ring[way * 4 + 3, o].astype(F32) * sand[o], axis=0, keepdims=True)
                     acc[s, d, pl.ds(o, 1)] = (term[:, :n] + term[:, n:]) * (1.0 / n)
     else:
@@ -307,7 +314,7 @@
             jax.ShapeDtypeStruct((ops, n // 2, 2 * n), BF16),
             jax.ShapeDtypeStruct((2, seps, half, n), F32),
         ),
-        in_specs=[pl.BlockSpec(memory_space=pltpu.SMEM)] + [vmem] * 4,
+        in_specs=[pl.BlockSpec(memory_space=pltpu.SMEM)] + [vmem] * 3 + [pl.BlockSpec(memory_space=pl.ANY)],
         out_specs=(vmem, vmem),
         scratch_shapes=[
             pltpu.VMEM((2, 3, nx + 2, ny, nz, n), BF16),
@@ -322,13 +329,15 @@
             pltpu.VMEM((spins * n, half * 2 * n), BF16),
             pltpu.VMEM((half, n, 2 * n), F32),
             pltpu.VMEM((2, seps, half, n), F32),
+            pltpu.VMEM(perams.shape, BF16),
+            pltpu.SemaphoreType.DMA,
             pltpu.SemaphoreType.DMA((half + 5,)),
             pltpu.SemaphoreType.DMA((half + 5,)),
-            pltpu.SemaphoreType.DMA((8, 4, 2)),
-            pltpu.SemaphoreType.DMA((8, 4, 2)),
+            pltpu.SemaphoreType.DMA((8, 4, half)),
+            pltpu.SemaphoreType.DMA((8, 4, half)),
         ],
         compiler_params=pltpu.CompilerParams(
-            collective_id=0, has_side_effects=True, vmem_limit_bytes=40 * 2**20
+            collective_id=0, has_side_effects=True, vmem_limit_bytes=48 * 2**20
         ),
         name="mesons",
     )(displacements, field, links, phases, perams)

time: 48.6 us -> 48.6 us (level)
  no operation moved by 1% of the time
where the time goes in v2:
time: 48.6 us; the launch traced here: 48.3 us
  Pallas kernels  40.2 us (83%)
  local copies, waits for them, and re-layouts  5.86 us (12%)
  other arithmetic  1.51 us (3%)
  between operations  0.69 us (1%)
    pallas_call x1, Pallas kernels, body(): pl.pallas_call(functools.partial(meson_kernel, count, norm), out_shape=(j...  40.2 us
    unnamed x7, local copies, waits for them, and re-layouts  3.94 us
    another operation x1, local copies, waits for them, and re-layouts, body(): links = jnp.transpose(links.reshape(54, nx, ny, nz), (1, 2, 3, 0))  1.24 us

profile of v2, /device:TPU:0, one launch (start us, length us, event | category | flops | bytes accessed | tf_op | source)
XLA Modules:
  0.0 48.3 jit_solution(16084152665405658442)
XLA Ops:
  0.7 0.7 %convert_element_type.24 = f32[8,3]{0,1:T(4,128)S(1)} convert(s32[8,3]{0,1:T(4,128)} %param.8) | non-fusion elementwise | flops 24 | bytes 192 | tf_op jit(solution)/shard_map/convert_element_type | solution.py:299
  1.4 0.1 multiply_multiply_fusion.1
  1.4 0.1 multiply_multiply_fusion
  1.5 1.2 %copy.11 = f32[54,4,4,16]{0,3,2,1:T(8,128)S(1)} copy(f32[54,4,4,16]{3,2,1,0:T(4,128)} %bitcast.19) | data formatting | bytes 110592 | tf_op jit(solution)/shard_map/reshape;squeeze | solution.py:293
  2.8 0.5 fusion.1
  3.2 0.1 pad_maximum_fusion.phase_ref
  3.3 0.0 copy-start
  3.4 1.6 %copy-done = bf16[1,8,4,128,256]{4,3,2,1,0:T(8,128)(2,1)S(1)} copy-done((bf16[1,8,4,128,256]{4,3,2,1,0:T(8,128)(2,1)S(1)}, bf16[1,8,4,128,256]{4,3,2,1,0:T(8,128)(2,1)}, u32[]{:S(2)}) %copy-start) | copy-done | bytes 2097176
  4.9 0.0 copy-start.1
  4.9 1.0 %copy-done.1 = bf16[1,2,3,4,4,16,128]{6,5,4,3,2,1,0:T(8,128)(2,1)S(1)} copy-done((bf16[1,2,3,4,4,16,128]{6,5,4,3,2,1,0:T(8,128)(2,1)S(1)}, bf16[1,2,3,4,4,16,128]{6,5,4,3,2,1,0:T(8,128)(2,1)}, u32[]{:S(2)}) %copy-start.1) | copy-done | bytes 393240
  5.9 0.0 copy-start.2
  5.9 0.7 %copy-done.2 = s32[8]{0:T(128)S(1)} copy-done((s32[8]{0:T(128)S(1)}, s32[8]{0:T(128)}, u32[]{:S(2)}) %copy-start.2) | copy-done | bytes 56
  6.6 40.2 %mesons.1 = (bf16[8,64,256]{2,1,0:T(8,128)(2,1)S(1)}, f32[2,8,4,128]{3,2,1,0:T(4,128)S(1)}) custom-call(s32[8]{0:T(128)S(1)} %copy-done.2, bf16[2,3,4,4,16,128]{5,4,3,2,1,0:T(8,128)(2,1)S(1)} %bitcast.17, f32[4,4,16,54]{3,2,1,0:T(8,128)S(1)} %bitcast.16, f32[4,4,16,16]{3,2,1,0:T(8,128)S(1)} %pad_maximum_fusion.phase_ref, bf16[8,4,128,256]{3,2,1,0:T(8,128)(2,1)S(1)} %bitcast.15), custom_call_target="tpu_custom_call" | custom-call | tf_op jit(solution)/shard_map/mesons/pallas_call | solution.py:311
  46.8 0.1 reduce_sum.9
  46.9 0.7 %copy.12 = f32[2,4,8]{2,1,0:T(4,128)} copy(f32[2,4,8]{1,2,0:T(8,128)S(1)} %bitcast.20) | data formatting | bytes 512 | tf_op jit(solution)/shard_map/transpose | solution.py:345
  47.6 0.7 %copy.15 = bf16[1,8,64,256]{3,2,1,0:T(8,128)(2,1)} copy(bf16[1,8,64,256]{3,2,1,0:T(8,128)(2,1)S(1)} %bitcast.18) | data formatting | bytes 524288
  (5 shorter events, 0.0 us)
Async XLA Ops:
  3.3 1.6 %copy-start = (bf16[1,8,4,128,256]{4,3,2,1,0:T(8,128)(2,1)S(1)}, bf16[1,8,4,128,256]{4,3,2,1,0:T(8,128)(2,1)}, u32[]{:S(2)}) copy-start(bf16[1,8,4,128,256]{4,3,2,1,0:T(8,128)(2,1)} %param.7) | copy-start | bytes 6291460
  4.9 1.0 %copy-start.1 = (bf16[1,2,3,4,4,16,128]{6,5,4,3,2,1,0:T(8,128)(2,1)S(1)}, bf16[1,2,3,4,4,16,128]{6,5,4,3,2,1,0:T(8,128)(2,1)}, u32[]{:S(2)}) copy-start(bf16[1,2,3,4,4,16,128]{6,5,4,3,2,1,0:T(8,128)(2,1)} %param.5) | copy-start | bytes 1179652
  5.9 0.7 %copy-start.2 = (s32[8]{0:T(128)S(1)}, s32[8]{0:T(128)}, u32[]{:S(2)}) copy-start(s32[8]{0:T(128)} %disp_ref.1) | copy-start | bytes 100

commit v3 on v2

--- a/solution.py
+++ b/solution.py
@@ -99,7 +99,7 @@
             cosine = spread(angles, o)
             sine = spread(angles, ops + o)
             for c in range(3):
-                vr, vi = v_ref[0, c, x, y].astype(F32), v_ref[1, c, x, y].astype(F32)
+                vr, vi = pad[0, c, x + 1, y].astype(F32), pad[1, c, x + 1, y].astype(F32)
                 left[o, c, i, :, :n] = (vr * cosine - vi * sine).astype(BF16)
                 left[o, c, i, :, n:] = (vr * sine + vi * cosine).astype(BF16)
         return carry
@@ -111,10 +111,13 @@
 
 def meson_kernel(
     count, norm, disp_ref, v_ref, link_ref, phase_ref, per_hbm, elem_ref, corr_ref,
-    pad, links, fields, left, part, got, own, rows_in, ring, mixed, sand, acc, per_ref, per_sem, pair_send, pair_recv, send_sem, recv_sem,
+    pad, links, fields, left, part, got, own, rows_in, ring, mixed, sand, acc, per_ref, per_sem, v_sem, pair_send, pair_recv, send_sem, recv_sem,
 ):
     seps, spins, n, wide = per_ref.shape
     fetch = pltpu.make_async_copy(per_hbm, per_ref, per_sem)
+    inner = pad.at[:, :, pl.ds(1, v_ref.shape[2])]
+    fetch_v = pltpu.make_async_copy(v_ref, inner, v_sem)
+    fetch_v.start()
     fetch.start()
     half = own.shape[0]
     mine_rows = elem_ref.shape[1]
@@ -158,8 +161,8 @@
         pair(v_ref.at[:, :, 0], pad.at[:, :, nx + 1], half + 3),
         pair(link_ref.at[nx - 1], links.at[0], half + 4),
     ]
-    pad[:, :, 1 : nx + 1] = v_ref[...]
     links[1:] = link_ref[...]
+    fetch_v.wait()
 
     def ready():
         for copy in halo:
@@ -173,13 +176,15 @@
         block = lax.dot_general(lhs, rhs, (((0,), (0,)), ((), ())), preferred_element_type=F32)
         return combine(block, n)
 
-    first = []
+    first = {}
+    middle = half // 2
+    order = [g + w * middle for g in range(middle) for w in range(2)]
 
     def project_other(o):
         part[o, :, :n], part[o, :, n:] = project(other * half + o)
-        first.append(pair(part.at[o], got.at[o], o))
-
-    project_other(0)
+        first[o] = pair(part.at[o], got.at[o], o)
+
+    project_other(order[0])
 
     if ringed:
         pieces = half
@@ -195,17 +200,22 @@
             )
 
     hops = {}
-    for o in range(half):
-        if o + 1 < half:
-            project_other(o + 1)
+    for at, o in enumerate(order):
+        if at + 1 < half:
+            project_other(order[at + 1])
         real, imag = project(s * half + o)
         first[o].wait_recv()
         own[o, :, :n] = ((real + got[o, :, :n]) * norm).astype(BF16)
         own[o, :, n:] = ((imag + got[o, :, n:]) * norm).astype(BF16)
-        if ringed and (o + 1) % size == 0:
-            for way in range(2):
-                hops[way, 0, o // size] = hop(way, 0, o // size)
-                hops[way, 0, o // size].start()
+        if ringed:
+            way = o // middle
+            hops[way, 0, o] = hop(way, 0, o)
+            hops[way, 0, o].start()
+    if ringed:
+        for o in range(half):
+            way = 1 - o // middle
+            hops[way, 0, o] = hop(way, 0, o)
+            hops[way, 0, o].start()
     if not ringed:
         for k in range(seps - 1):
             hops[k] = pltpu.make_async_remote_copy(
@@ -243,12 +253,13 @@
     contract(0, own)
     if ringed:
         for k in range(1, 5):
-            for g in range(pieces):
+            for j in range(pieces):
                 for way in range(2):
+                    g = (j + way * middle) % half
                     if (way, k - 1, g) not in hops or k == 4:
                         continue
                     hops[way, k - 1, g].wait_recv()
-                    if k < 3 or g // 2 == way:
+                    if k < 3 or g // middle == way:
                         hops[way, k, g] = hop(way, k, g)
                         hops[way, k, g].start()
             if k < 4:
@@ -261,7 +272,7 @@
                 d = (t - at_place(place + 4) + 8) % 8
                 sandwich(d)
                 for o in range(half):
-                    way = o // 2
+                    way = o // middle
                     hops[way, 3, o].wait_recv()
                     term = jnp.sum(ring[way * 4 + 3, o].astype(F32) * sand[o], axis=0, keepdims=True)
                     acc[s, d, pl.ds(o, 1)] = (term[:, :n] + term[:, n:]) * (1.0 / n)
@@ -275,7 +286,7 @@
     elem_ref[pl.ds(other * half, half)] = rows_in[...]
     for copy in hops.values():
         copy.wait_send()
-    for copy in halo + first:
+    for copy in halo + list(first.values()):
         copy.wait_send()
     rows_copy.wait_send()
     last.wait()
@@ -304,6 +315,7 @@
     phases = jnp.concatenate([jnp.cos(angle), jnp.sin(angle)], axis=-1)
 
     vmem = pl.BlockSpec(memory_space=pltpu.VMEM)
+    hbm = pl.BlockSpec(memory_space=pltpu.HBM)
     perams = perambulators[0]
     seps, spins = perams.shape[:2]
     half = ops // 2
@@ -314,7 +326,7 @@
             jax.ShapeDtypeStruct((ops, n // 2, 2 * n), BF16),
             jax.ShapeDtypeStruct((2, seps, half, n), F32),
         ),
-        in_specs=[pl.BlockSpec(memory_space=pltpu.SMEM)] + [vmem] * 3 + [pl.BlockSpec(memory_space=pl.ANY)],
+        in_specs=[pl.BlockSpec(memory_space=pltpu.SMEM), hbm, vmem, vmem, hbm],
         out_specs=(vmem, vmem),
         scratch_shapes=[
             pltpu.VMEM((2, 3, nx + 2, ny, nz, n), BF16),
@@ -331,6 +343,7 @@
             pltpu.VMEM((2, seps, half, n), F32),
             pltpu.VMEM(perams.shape, BF16),
             pltpu.SemaphoreType.DMA,
+            pltpu.SemaphoreType.DMA,
             pltpu.SemaphoreType.DMA((half + 5,)),
             pltpu.SemaphoreType.DMA((half + 5,)),
             pltpu.SemaphoreType.DMA((8, 4, half)),

time: 48.6 us -> 48.3 us (level)
  no operation moved by 1% of the time
where the time goes in v3:
time: 48.3 us; the launch traced here: 48 us
  Pallas kernels  39.9 us (83%)
  local copies, waits for them, and re-layouts  5.86 us (12%)
  other arithmetic  1.51 us (3%)
  between operations  0.69 us (1%)
    pallas_call x1, Pallas kernels, body(): pl.pallas_call(functools.partial(meson_kernel, count, norm), out_shape=(j...  39.9 us
    unnamed x7, local copies, waits for them, and re-layouts  3.94 us
    another operation x1, local copies, waits for them, and re-layouts, body(): links = jnp.transpose(links.reshape(54, nx, ny, nz), (1, 2, 3, 0))  1.24 us

profile of v3, /device:TPU:0, one launch (start us, length us, event | category | flops | bytes accessed | tf_op | source)
XLA Modules:
  0.0 48.0 jit_solution(16916778914392190428)
XLA Ops:
  0.7 0.7 %convert_element_type.24 = f32[8,3]{0,1:T(4,128)S(1)} convert(s32[8,3]{0,1:T(4,128)} %param.8) | non-fusion elementwise | flops 24 | bytes 192 | tf_op jit(solution)/shard_map/convert_element_type | solution.py:310
  1.4 0.1 multiply_multiply_fusion.1
  1.4 0.1 multiply_multiply_fusion
  1.5 1.2 %copy.11 = f32[54,4,4,16]{0,3,2,1:T(8,128)S(1)} copy(f32[54,4,4,16]{3,2,1,0:T(4,128)} %bitcast.19) | data formatting | bytes 110592 | tf_op jit(solution)/shard_map/reshape;squeeze | solution.py:304
  2.8 0.5 fusion.1
  3.2 0.1 pad_maximum_fusion.phase_ref
  3.3 0.0 copy-start
  3.4 1.6 %copy-done = bf16[1,8,4,128,256]{4,3,2,1,0:T(8,128)(2,1)S(1)} copy-done((bf16[1,8,4,128,256]{4,3,2,1,0:T(8,128)(2,1)S(1)}, bf16[1,8,4,128,256]{4,3,2,1,0:T(8,128)(2,1)}, u32[]{:S(2)}) %copy-start) | copy-done | bytes 2097176
  4.9 0.0 copy-start.1
  4.9 1.0 %copy-done.1 = bf16[1,2,3,4,4,16,128]{6,5,4,3,2,1,0:T(8,128)(2,1)S(1)} copy-done((bf16[1,2,3,4,4,16,128]{6,5,4,3,2,1,0:T(8,128)(2,1)S(1)}, bf16[1,2,3,4,4,16,128]{6,5,4,3,2,1,0:T(8,128)(2,1)}, u32[]{:S(2)}) %copy-start.1) | copy-done | bytes 393240
  5.9 0.0 copy-start.2
  5.9 0.7 %copy-done.2 = s32[8]{0:T(128)S(1)} copy-done((s32[8]{0:T(128)S(1)}, s32[8]{0:T(128)}, u32[]{:S(2)}) %copy-start.2) | copy-done | bytes 56
  6.6 39.9 %mesons.1 = (bf16[8,64,256]{2,1,0:T(8,128)(2,1)S(1)}, f32[2,8,4,128]{3,2,1,0:T(4,128)S(1)}) custom-call(s32[8]{0:T(128)S(1)} %copy-done.2, bf16[2,3,4,4,16,128]{5,4,3,2,1,0:T(8,128)(2,1)S(1)} %bitcast.17, f32[4,4,16,54]{3,2,1,0:T(8,128)S(1)} %bitcast.16, f32[4,4,16,16]{3,2,1,0:T(8,128)S(1)} %pad_maximum_fusion.phase_ref, bf16[8,4,128,256]{3,2,1,0:T(8,128)(2,1)S(1)} %bitcast.15), custom_call_target="tpu_custom_call" | custom-call | tf_op jit(solution)/shard_map/mesons/pallas_call | solution.py:323
  46.5 0.1 reduce_sum.9
  46.6 0.7 %copy.12 = f32[2,4,8]{2,1,0:T(4,128)} copy(f32[2,4,8]{1,2,0:T(8,128)S(1)} %bitcast.20) | data formatting | bytes 512 | tf_op jit(solution)/shard_map/transpose | solution.py:358
  47.3 0.7 %copy.15 = bf16[1,8,64,256]{3,2,1,0:T(8,128)(2,1)} copy(bf16[1,8,64,256]{3,2,1,0:T(8,128)(2,1)S(1)} %bitcast.18) | data formatting | bytes 524288
  (5 shorter events, 0.0 us)
Async XLA Ops:
  3.3 1.6 %copy-start = (bf16[1,8,4,128,256]{4,3,2,1,0:T(8,128)(2,1)S(1)}, bf16[1,8,4,128,256]{4,3,2,1,0:T(8,128)(2,1)}, u32[]{:S(2)}) copy-start(bf16[1,8,4,128,256]{4,3,2,1,0:T(8,128)(2,1)} %param.7) | copy-start | bytes 6291460
  4.9 1.0 %copy-start.1 = (bf16[1,2,3,4,4,16,128]{6,5,4,3,2,1,0:T(8,128)(2,1)S(1)}, bf16[1,2,3,4,4,16,128]{6,5,4,3,2,1,0:T(8,128)(2,1)}, u32[]{:S(2)}) copy-start(bf16[1,2,3,4,4,16,128]{6,5,4,3,2,1,0:T(8,128)(2,1)} %param.5) | copy-start | bytes 1179652
  5.9 0.7 %copy-start.2 = (s32[8]{0:T(128)S(1)}, s32[8]{0:T(128)}, u32[]{:S(2)}) copy-start(s32[8]{0:T(128)} %disp_ref.1) | copy-start | bytes 100

commit v4 on v3

--- a/solution.py
+++ b/solution.py
@@ -246,7 +246,7 @@
     def contract(d, block):
         for o in range(half):
             term = jnp.sum(block[o].astype(F32) * sand[o], axis=0, keepdims=True)
-            acc[s, d, pl.ds(o, 1)] = (term[:, :n] + term[:, n:]) * (1.0 / n)
+            acc[s, o, pl.ds(d, 1)] = (term[:, :n] + term[:, n:]) * (1.0 / n)
 
     fetch.wait()
     sandwich(0)
@@ -275,7 +275,7 @@
                     way = o // middle
                     hops[way, 3, o].wait_recv()
                     term = jnp.sum(ring[way * 4 + 3, o].astype(F32) * sand[o], axis=0, keepdims=True)
-                    acc[s, d, pl.ds(o, 1)] = (term[:, :n] + term[:, n:]) * (1.0 / n)
+                    acc[s, o, pl.ds(d, 1)] = (term[:, :n] + term[:, n:]) * (1.0 / n)
     else:
         for k in range(seps - 1):
             sandwich(k + 1)
@@ -324,7 +324,7 @@
         functools.partial(meson_kernel, count, norm),
         out_shape=(
             jax.ShapeDtypeStruct((ops, n // 2, 2 * n), BF16),
-            jax.ShapeDtypeStruct((2, seps, half, n), F32),
+            jax.ShapeDtypeStruct((2, half, seps, n), F32),
         ),
         in_specs=[pl.BlockSpec(memory_space=pltpu.SMEM), hbm, vmem, vmem, hbm],
         out_specs=(vmem, vmem),
@@ -340,7 +340,7 @@
             pltpu.VMEM((8, half, n, 2 * n), BF16),
             pltpu.VMEM((spins * n, half * 2 * n), BF16),
             pltpu.VMEM((half, n, 2 * n), F32),
-            pltpu.VMEM((2, seps, half, n), F32),
+            pltpu.VMEM((2, half, seps, n), F32),
             pltpu.VMEM(perams.shape, BF16),
             pltpu.SemaphoreType.DMA,
             pltpu.SemaphoreType.DMA,
@@ -354,8 +354,7 @@
         ),
         name="mesons",
     )(displacements, field, links, phases, perams)
-    corr = jnp.sum(corr, axis=-1)
-    corr = jnp.transpose(corr, (0, 2, 1)).reshape(ops, 1, seps)
+    corr = jnp.sum(corr, axis=-1).reshape(ops, 1, seps)
     return (elementals[None], corr)
 
 

time: 48.3 us -> 48.2 us (level)
  local copies, waits for them, and re-layouts: 5.86 us -> 5.19 us
  other arithmetic: 1.51 us -> 2.11 us
    transpose x1 -> x0, local copies, waits for them, and re-layouts: 0.68 us -> none  [body(): corr = jnp.transpose(corr, (0, 2, 1)).reshape(ops, 1, seps)]
    reduce_sum x1, other arithmetic: 0.09 us -> 0.68 us  [body(): corr = jnp.sum(corr, axis=-1).reshape(ops, 1, seps)]
where the time goes in v4:
time: 48.2 us; the launch traced here: 47.9 us
  Pallas kernels  39.9 us (83%)
  local copies, waits for them, and re-layouts  5.19 us (11%)
  other arithmetic  2.11 us (4%)
  between operations  0.69 us (1%)
    pallas_call x1, Pallas kernels, body(): pl.pallas_call(functools.partial(meson_kernel, count, norm), out_shape=(j...  39.9 us
    unnamed x7, local copies, waits for them, and re-layouts  3.94 us
    another operation x1, local copies, waits for them, and re-layouts, body(): links = jnp.transpose(links.reshape(54, nx, ny, nz), (1, 2, 3, 0))  1.24 us

profile of v4, /device:TPU:0, one launch (start us, length us, event | category | flops | bytes accessed | tf_op | source)
XLA Modules:
  0.0 47.9 jit_solution(12435312120684241465)
XLA Ops:
  0.7 0.7 %convert_element_type.24 = f32[8,3]{0,1:T(4,128)S(1)} convert(s32[8,3]{0,1:T(4,128)} %param.8) | non-fusion elementwise | flops 24 | bytes 192 | tf_op jit(solution)/shard_map/convert_element_type | solution.py:310
  1.4 0.1 multiply_multiply_fusion.1
  1.4 0.1 multiply_multiply_fusion
  1.5 1.2 %copy.9 = f32[54,4,4,16]{0,3,2,1:T(8,128)S(1)} copy(f32[54,4,4,16]{3,2,1,0:T(4,128)} %bitcast.18) | data formatting | bytes 110592 | tf_op jit(solution)/shard_map/reshape;squeeze | solution.py:304
  2.8 0.5 fusion.1
  3.2 0.1 pad_maximum_fusion.phase_ref
  3.3 0.0 copy-start
  3.4 1.6 %copy-done = bf16[1,8,4,128,256]{4,3,2,1,0:T(8,128)(2,1)S(1)} copy-done((bf16[1,8,4,128,256]{4,3,2,1,0:T(8,128)(2,1)S(1)}, bf16[1,8,4,128,256]{4,3,2,1,0:T(8,128)(2,1)}, u32[]{:S(2)}) %copy-start) | copy-done | bytes 2097176
  4.9 0.0 copy-start.1
  4.9 1.0 %copy-done.1 = bf16[1,2,3,4,4,16,128]{6,5,4,3,2,1,0:T(8,128)(2,1)S(1)} copy-done((bf16[1,2,3,4,4,16,128]{6,5,4,3,2,1,0:T(8,128)(2,1)S(1)}, bf16[1,2,3,4,4,16,128]{6,5,4,3,2,1,0:T(8,128)(2,1)}, u32[]{:S(2)}) %copy-start.1) | copy-done | bytes 393240
  5.9 0.0 copy-start.2
  5.9 0.7 %copy-done.2 = s32[8]{0:T(128)S(1)} copy-done((s32[8]{0:T(128)S(1)}, s32[8]{0:T(128)}, u32[]{:S(2)}) %copy-start.2) | copy-done | bytes 56
  6.6 39.9 %mesons.1 = (bf16[8,64,256]{2,1,0:T(8,128)(2,1)S(1)}, f32[2,4,8,128]{3,2,1,0:T(8,128)S(1)}) custom-call(s32[8]{0:T(128)S(1)} %copy-done.2, bf16[2,3,4,4,16,128]{5,4,3,2,1,0:T(8,128)(2,1)S(1)} %bitcast.16, f32[4,4,16,54]{3,2,1,0:T(8,128)S(1)} %bitcast.15, f32[4,4,16,16]{3,2,1,0:T(8,128)S(1)} %pad_maximum_fusion.phase_ref, bf16[8,4,128,256]{3,2,1,0:T(8,128)(2,1)S(1)} %bitcast.14), custom_call_target="tpu_custom_call" | custom-call | tf_op jit(solution)/shard_map/mesons/pallas_call | solution.py:323
  46.5 0.7 %reduce_sum.9 = f32[2,4,8]{2,1,0:T(4,128)} reduce(f32[2,4,8,128]{3,2,1,0:T(8,128)S(1)} %get-tuple-element.5, f32[]{:T(128)} %constant.18.clone.1), dimensions={3}, to_apply=%region_0.0 | reduce | flops 8128 | bytes 33028 | tf_op jit(solution)/shard_map/reduce_sum | solution.py:357
  47.2 0.7 %copy.12 = bf16[1,8,64,256]{3,2,1,0:T(8,128)(2,1)} copy(bf16[1,8,64,256]{3,2,1,0:T(8,128)(2,1)S(1)} %bitcast.17) | data formatting | bytes 524288
  (5 shorter events, 0.0 us)
Async XLA Ops:
  3.3 1.6 %copy-start = (bf16[1,8,4,128,256]{4,3,2,1,0:T(8,128)(2,1)S(1)}, bf16[1,8,4,128,256]{4,3,2,1,0:T(8,128)(2,1)}, u32[]{:S(2)}) copy-start(bf16[1,8,4,128,256]{4,3,2,1,0:T(8,128)(2,1)} %param.7) | copy-start | bytes 6291460
  4.9 1.0 %copy-start.1 = (bf16[1,2,3,4,4,16,128]{6,5,4,3,2,1,0:T(8,128)(2,1)S(1)}, bf16[1,2,3,4,4,16,128]{6,5,4,3,2,1,0:T(8,128)(2,1)}, u32[]{:S(2)}) copy-start(bf16[1,2,3,4,4,16,128]{6,5,4,3,2,1,0:T(8,128)(2,1)} %param.5) | copy-start | bytes 1179652
  5.9 0.7 %copy-start.2 = (s32[8]{0:T(128)S(1)}, s32[8]{0:T(128)}, u32[]{:S(2)}) copy-start(s32[8]{0:T(128)} %disp_ref.1) | copy-start | bytes 100
